TPU v7x, 32 devices: a whole 2x2x4 slice. The times are simulated.
32 devices in a mesh: ctx: 8 (over z, core), exp: 4 (over y, x).
Axes of the slice: x: 2, y: 2, z: 4, core: 2. Of those that a mesh axis runs over, the one named last changes fastest.
Arguments:
- queries: bfloat16 [4, 2048, 2048], P('exp', 'ctx'), may hold values from -64 to 64
- keys: bfloat16 [4, 2048, 256], P('exp', 'ctx'), may hold values from -6 to 6
- values: bfloat16 [4, 2048, 256], P('exp', 'ctx'), may hold values from -6 to 6
- hidden_in: bfloat16 [4, 2048, 2048], P('exp', 'ctx'), may hold values from -60 to 60
- out_proj: bfloat16 [2048, 2048], replicated, may hold values from -1.5 to 1.5
- norm_gain: float32 [2048], replicated, may hold values from 0.1 to 1.9
- route_ids: int32 [4, 2048, 8], P('exp', 'ctx'), may hold values from 0 to 31, all different within a row; in each aligned block of 256 rows (0 to 255, 256 to 511, ..., all dimensions but the last counted through in order) at most 128 rows name the same one
- route_scores: float32 [4, 2048, 8], P('exp', 'ctx'), may hold values from -310 to 310
- expert_weights: bfloat16 [32, 3, 2048, 768], P(('ctx', 'exp')), may hold values from -0.25 to 0.25
Outputs:
- residual_out: bfloat16 [4, 2048, 2048], P('exp', 'ctx')
- layer_out: bfloat16 [4, 2048, 2048], P('exp', 'ctx')
Inputs may be any that keep to these rules, and one draw needn't show every extreme that they name: `route_ids`: each row names 8 different experts. In each aligned block of 256 rows (the rows of one device) no expert is named by more than 128 rows.
All inputs are finite; a program needn't handle non-finite values.
Results may differ from a plain program's by a relative error of at most 0.023.
Values may be sent and summed in bfloat16 or wider, within the bound.
A program may use at most 192 MiB of HBM per device.

v0:
```python
import math

import jax
import jax.numpy as jnp
from jax import lax
from jax.sharding import PartitionSpec as P

D = 2048
HEADS = 16
KV_HEADS = 2
HEAD_DIM = 128
TOP = 8


def expert_rows(rows, weights):
    gate_part = jnp.dot(rows, weights[0], preferred_element_type=jnp.float32)
    upper_part = jnp.dot(rows, weights[1], preferred_element_type=jnp.float32)
    hidden_rows = (jax.nn.silu(gate_part) * upper_part).astype(jnp.bfloat16)
    result = lax.dot_general(
        hidden_rows, weights[2], (((1,), (1,)), ((), ())), preferred_element_type=jnp.float32
    )
    return result.astype(jnp.bfloat16)


def on_device(
    queries, keys, values, hidden_in, out_proj, norm_gain, route_ids, route_scores, expert_weights
):
    tok_rows = queries.shape[1]
    group_size = HEADS // KV_HEADS
    score_scale = 1.0 / math.sqrt(HEAD_DIM)
    query_heads = queries[0].reshape(tok_rows, KV_HEADS, group_size, HEAD_DIM)
    first_row = lax.axis_index("ctx") * tok_rows
    query_pos = first_row + jnp.arange(tok_rows, dtype=jnp.int32)
    last_row = first_row + tok_rows - 1
    start_state = (
        jnp.full((tok_rows, KV_HEADS, group_size), -1e30, jnp.float32),
        jnp.zeros((tok_rows, KV_HEADS, group_size), jnp.float32),
        jnp.zeros((tok_rows, KV_HEADS, group_size, HEAD_DIM), jnp.float32),
    )
    running = start_state
    key_piece = lax.all_gather(keys[0], "ctx", axis=0, tiled=True)
    value_piece = lax.all_gather(values[0], "ctx", axis=0, tiled=True)
    piece_rows = key_piece.shape[0]
    absorb_block_rows = math.gcd(piece_rows, 512)

    def one_block(index, running):
        block_start = index * absorb_block_rows

        def compute(running):
            running_max, denom, accum = running
            key_rows = lax.dynamic_slice_in_dim(
                key_piece, block_start, absorb_block_rows, 0
            ).reshape(absorb_block_rows, KV_HEADS, HEAD_DIM)
            value_rows = lax.dynamic_slice_in_dim(
                value_piece, block_start, absorb_block_rows, 0
            ).reshape(absorb_block_rows, KV_HEADS, HEAD_DIM)
            scores = (
                jnp.einsum(
                    "tgjd,ngd->tgjn", query_heads, key_rows, preferred_element_type=jnp.float32
                )
                * score_scale
            )
            key_pos = block_start + jnp.arange(absorb_block_rows, dtype=jnp.int32)
            visible = (key_pos[None, :] <= query_pos[:, None])[:, None, None, :]
            scores = jnp.where(visible, scores, -1e30)
            new_max = jnp.maximum(running_max, scores.max(-1))
            exps = jnp.where(visible, jnp.exp(scores - new_max[..., None]), 0.0)
            rescale = jnp.exp(running_max - new_max)
            denom = denom * rescale + exps.sum(-1)
            added = jnp.einsum(
                "tgjn,ngd->tgjd",
                exps.astype(jnp.bfloat16),
                value_rows,
                preferred_element_type=jnp.float32,
            )
            accum = accum * rescale[..., None] + added
            return (new_max, denom, accum)

        def unchanged(running):
            return running

        return lax.cond(block_start <= last_row, compute, unchanged, running)

    running_max, denom, accum = lax.fori_loop(
        0, piece_rows // absorb_block_rows, one_block, running
    )
    attended = (accum / denom[..., None]).reshape(tok_rows, HEADS * HEAD_DIM).astype(jnp.bfloat16)
    projected = jnp.dot(attended, out_proj, preferred_element_type=jnp.float32)
    residual = (hidden_in[0].astype(jnp.float32) + projected).astype(jnp.bfloat16)
    resid_f = residual.astype(jnp.float32)
    normed = (
        resid_f * lax.rsqrt(jnp.mean(resid_f * resid_f, -1, keepdims=True) + 1e-06) * norm_gain
    ).astype(jnp.bfloat16)
    gates = jax.nn.softmax(route_scores[0], -1)
    n_ctx = lax.axis_size("ctx")
    n_exp = lax.axis_size("exp")
    n_experts = n_ctx * n_exp
    capacity = 2 * tok_rows * TOP // n_experts
    expert_ids = route_ids[0].reshape(-1)
    one_hot = (expert_ids[:, None] == jnp.arange(n_experts, dtype=jnp.int32)[None, :]).astype(
        jnp.int32
    )
    earlier = jnp.cumsum(one_hot, 0) - one_hot
    ranks = jnp.sum(earlier * one_hot, 1)
    my_counts = jnp.sum(one_hot, 0)
    pair_slots = expert_ids * capacity + ranks
    outgoing = (
        jnp.zeros((n_experts * capacity, D), jnp.bfloat16)
        .at[pair_slots]
        .set(jnp.repeat(normed, TOP, axis=0))
    )
    local_weights = expert_weights[0]
    count_rows = my_counts.astype(jnp.bfloat16)
    incoming, count_in = (
        lax.all_to_all(
            outgoing.reshape(n_experts, capacity, D),
            ("ctx", "exp"),
            split_axis=0,
            concat_axis=0,
            tiled=True,
        ),
        lax.all_to_all(
            count_rows.reshape(n_experts, 1),
            ("ctx", "exp"),
            split_axis=0,
            concat_axis=0,
            tiled=True,
        ),
    )
    incoming = incoming.reshape(n_experts * capacity, D)
    column = count_in.reshape(n_experts).astype(jnp.int32)
    ends = jnp.cumsum(column)
    starts = ends - column
    received_rows = ends[-1]
    packed_pos = jnp.arange(n_experts * capacity, dtype=jnp.int32)
    source = jnp.minimum(
        jnp.sum((packed_pos[:, None] >= ends[None, :]).astype(jnp.int32), 1), n_experts - 1
    )
    within = packed_pos - starts[source]
    live = packed_pos < received_rows
    anchor = jnp.where(live, source * capacity + within, 0)
    packed = incoming[anchor]
    block_rows = math.gcd(n_experts * capacity, 512)

    def serve(index, results):
        rows = lax.dynamic_slice_in_dim(packed, index * block_rows, block_rows, 0)
        return lax.dynamic_update_slice_in_dim(
            results, expert_rows(rows, local_weights), index * block_rows, 0
        )

    turns = (received_rows + block_rows - 1) // block_rows
    served = lax.fori_loop(0, turns, serve, jnp.zeros((n_experts * capacity, D), jnp.bfloat16))
    target = jnp.where(live, anchor, n_experts * capacity)
    answers = jnp.zeros((n_experts * capacity, D), jnp.bfloat16).at[target].set(served, mode="drop")
    returned = lax.all_to_all(
        answers.reshape(n_experts, capacity, D),
        ("ctx", "exp"),
        split_axis=0,
        concat_axis=0,
        tiled=True,
    )
    returned = returned.reshape(n_experts * capacity, D)
    pair_out = returned[pair_slots].reshape(tok_rows, TOP, D)
    mixture = jnp.sum(gates[:, :, None] * pair_out.astype(jnp.float32), 1)
    layer_out = (resid_f + mixture).astype(jnp.bfloat16)
    return (residual[None], layer_out[None])


def solution(mesh):
    return jax.shard_map(
        on_device,
        mesh=mesh,
        in_specs=(
            P("exp", "ctx", None),
            P("exp", "ctx", None),
            P("exp", "ctx", None),
            P("exp", "ctx", None),
            P(),
            P(),
            P("exp", "ctx", None),
            P("exp", "ctx", None),
            P(("ctx", "exp"), None, None, None),
        ),
        out_specs=(P("exp", "ctx", None), P("exp", "ctx", None)),
        check_vma=False,
    )
```

profile of v0, /device:TPU:0, one launch (start us, length us, event | category | flops | bytes accessed | tf_op | source)
XLA Modules:
  0.0 1113.8 jit_solution(16866196699617416947)
XLA Ops:
  7.2 1.7 copy.58
  8.9 1.7 copy.60
  11.7 9.1 reduce-window.11
  22.4 7.3 all-to-all-start
  29.7 1.5 copy.59
  32.9 4.2 all-gather.5.cloned.1.call-done
  37.0 25.1 %all-gather.7.cloned.1.call-done = bf16[1,2048,256]{1,2,0:T(8,128)(2,1)} async-done(((bf16[1,256,256]{1,2,0:T(8,128)(2,1)}), bf16[1,2048,256]{1,2,0:T(8,128)(2,1)}) %all-gather.7.cloned.1.call-update) | async-done | bytes 1048592 | tf_op jit(solution)/shard_map/all_gather | solution.py:42
  62.4 7.7 while.29
  62.4 7.4 conditional.3
  63.7 1.5 fusion.2
  65.2 2.0 fusion.4
  67.3 2.6 bitcast_add_fusion
  70.3 6.1 fusion.51
  77.7 21.7 %scatter_custom_fusion = bf16[4096,2048]{1,0:T(8,128)(2,1)} fusion(s32[2048]{0:T(1024)S(1)} %bitcast.156, bf16[]{:T(256)} %constant.95.clone.1, bf16[256,2048]{1,0:T(8,128)(2,1)S(1)} %fusion.53), kind=kCustom, calls=%fused_computation.43 | custom fusion | bytes 17825794 | tf_op jit(solution)/shard_map/scatter | solution.py:110
  99.3 25.8 %all-to-all-start.1 = ((bf16[32,128,2048]{2,1,0:T(8,128)(2,1)}), bf16[32,128,2048]{2,1,0:T(8,128)(2,1)}, u32[]{:S(2)}, u32[]{:S(2)}) async-start(bf16[32,128,2048]{2,1,0:T(8,128)(2,1)} %bitcast.137), calls=%async_computation.1 | async-start | bytes 33554432 | tf_op jit(solution)/shard_map/all_to_all | solution.py:115
  128.9 4.1 compare_select_fusion.3
  134.3 15.6 %select_select_fusion = s32[4096]{0:T(1024)S(1)} fusion(pred[4096]{0:T(1024)(128)(4,1)S(1)} %get-tuple-element.314, pred[4096]{0:T(1024)(128)(4,1)S(1)} %get-tuple-element.313, pred[4096]{0:T(1024)(128)(4,1)S(1)} %get-tuple-element.312, pred[4096]{0:T(1024)(128)(4,1)S(1)} %get-tuple-element.311, pred[4096]{0:T(1024)(128)(4,1)S(1)} %get-tuple-element.310, ...), kind=kLoop, calls=%fused_computation.108 | loop fusion | flops 102400 | bytes 135268 | tf_op jit(solution)/shard_map/gather | solution.py:139
  151.3 356.6 %all-to-all-done.1 = bf16[32,128,2048]{2,1,0:T(8,128)(2,1)} async-done(((bf16[32,128,2048]{2,1,0:T(8,128)(2,1)}), bf16[32,128,2048]{2,1,0:T(8,128)(2,1)}, u32[]{:S(2)}, u32[]{:S(2)}) %all-to-all-start.1) | async-done | bytes 16777248 | tf_op jit(solution)/shard_map/all_to_all | solution.py:115
  507.9 39.3 %gather_fusion = bf16[4096,2048]{1,0:T(8,128)(2,1)} fusion(bf16[4096,2048]{1,0:T(8,128)(2,1)} %bitcast.63, s32[4096]{0:T(1024)S(1)} %broadcast_clamp_fusion), kind=kCustom, calls=%fused_computation | custom fusion | bytes 33570816 | tf_op jit(solution)/shard_map/gather | solution.py:142
  547.2 6.0 broadcast.215
  553.2 39.4 %while.28 = (s32[]{:T(128)}, bf16[4096,2048]{1,0:T(8,128)(2,1)}, s32[]{:T(128)}, bf16[4096,2048]{1,0:T(8,128)(2,1)}, bf16[3,2048,768]{2,1,0:T(8,128)(2,1)}, /*index=5*/s32[]{:T(128)}, s32[]{:T(128)}, s32[]{:T(128)}, s32[]{:T(128)}) while((s32[]{:T(128)}, bf16[4096,2048]{1,0:T(8,128)(2,1)}, s32[]{:T(128)}, bf16[4096,2048]{1,0:T(8,128)(2,1)}, ...), condition=%wide.region_17.18_spmd, body=%wide.region_16.17_spmd.sunk | while | flops 4835246080 | bytes 18875544 | solution.py:152
  553.2 4.3 fusion.81
  557.5 8.8 fusion.82
  566.3 4.3 fusion.81
  570.6 8.7 fusion.82
  579.3 4.3 fusion.81
  583.6 8.8 fusion.82
  592.6 33.4 %scatter_custom_fusion.1 = bf16[4096,2048]{1,0:T(8,128)(2,1)} fusion(s32[4096]{0:T(1024)S(1)} %bitcast.158, bf16[4096,2048]{1,0:T(8,128)(2,1)} %get-tuple-element.226, bf16[]{:T(256)} %constant.95.clone.1), kind=kCustom, calls=%fused_computation.45 | custom fusion | bytes 16777728 | tf_op jit(solution)/shard_map/scatter | solution.py:154
  626.0 61.0 %all-to-all-start.2 = ((bf16[32,128,2048]{2,1,0:T(8,128)(2,1)}), bf16[32,128,2048]{2,1,0:T(8,128)(2,1)}, u32[]{:S(2)}, u32[]{:S(2)}) async-start(bf16[32,128,2048]{2,1,0:T(8,128)(2,1)} %bitcast.138), calls=%async_computation.2 | async-start | bytes 33554432 | tf_op jit(solution)/shard_map/all_to_all | solution.py:155
  687.2 382.6 %all-to-all-done.2 = bf16[32,128,2048]{2,1,0:T(8,128)(2,1)} async-done(((bf16[32,128,2048]{2,1,0:T(8,128)(2,1)}), bf16[32,128,2048]{2,1,0:T(8,128)(2,1)}, u32[]{:S(2)}, u32[]{:S(2)}) %all-to-all-start.2) | async-done | bytes 16777248 | tf_op jit(solution)/shard_map/all_to_all | solution.py:155
  1069.7 24.3 %gather_fusion.1 = bf16[2048,2048]{1,0:T(8,128)(2,1)} fusion(bf16[4096,2048]{1,0:T(8,128)(2,1)} %bitcast.67, s32[2048]{0:T(1024)S(1)} %broadcast_clamp_fusion.1), kind=kCustom, calls=%fused_computation.1 | custom fusion | bytes 16785408 | tf_op jit(solution)/shard_map/gather | solution.py:163
  1094.0 11.2 %fusion.43 = f32[256,2048]{1,0:T(8,128)S(1)} fusion(bf16[2048,2048]{1,0:T(8,128)(2,1)} %gather_fusion.1, f32[256,8]{1,0:T(8,128)S(1)} %copy.62), kind=kLoop, calls=%fused_computation.42 | loop fusion | flops 12058624 | bytes 10493952 | tf_op jit(solution)/shard_map/reduce_sum | solution.py:164
  (69 shorter events, 14.5 us)
Async XLA Ops:
  7.2 29.9 %all-gather.5.cloned.1.call-start = ((), (), s32[]{:S(2)}) async-start(), calls=%async_computation.3 | async-start | bytes 1179648 | tf_op jit(solution)/shard_map/all_gather | solution.py:41
  8.9 53.3 %all-gather.7.cloned.1.call-start = ((), (), s32[]{:S(2)}) async-start(), calls=%async_computation.4 | async-start | bytes 1179648 | tf_op jit(solution)/shard_map/all_gather | solution.py:42
  22.4 76.9 %all-to-all-start = ((bf16[32,1,1]{2,1,0:T(2,128)(2,1)}), bf16[32,1,1]{2,1,0:T(2,128)(2,1)S(1)}, u32[]{:S(2)}, u32[]{:S(2)}) async-start(bf16[32,1,1]{2,1,0:T(2,128)(2,1)} %copy.64), calls=%async_computation | async-start | bytes 32768 | tf_op jit(solution)/shard_map/all_to_all | solution.py:122
  70.3 7.1 copy-start.3
  76.4 1.0 copy-start
  99.3 408.6 %all-to-all-start.1 = ((bf16[32,128,2048]{2,1,0:T(8,128)(2,1)}), bf16[32,128,2048]{2,1,0:T(8,128)(2,1)}, u32[]{:S(2)}, u32[]{:S(2)}) async-start(bf16[32,128,2048]{2,1,0:T(8,128)(2,1)} %bitcast.137), calls=%async_computation.1 | async-start | bytes 33554432 | tf_op jit(solution)/shard_map/all_to_all | solution.py:115
  626.0 61.0 %copy-start.2 = (f32[1,256,8]{1,2,0:T(8,128)S(1)}, f32[1,256,8]{1,2,0:T(8,128)}, u32[]{:S(2)}) copy-start(f32[1,256,8]{1,2,0:T(8,128)} %param.22) | copy-start | bytes 24580
  626.0 443.8 %all-to-all-start.2 = ((bf16[32,128,2048]{2,1,0:T(8,128)(2,1)}), bf16[32,128,2048]{2,1,0:T(8,128)(2,1)}, u32[]{:S(2)}, u32[]{:S(2)}) async-start(bf16[32,128,2048]{2,1,0:T(8,128)(2,1)} %bitcast.138), calls=%async_computation.2 | async-start | bytes 33554432 | tf_op jit(solution)/shard_map/all_to_all | solution.py:155
  1094.0 11.2 %copy-start.1 = (bf16[256,2048]{1,0:T(8,128)(2,1)S(1)}, bf16[256,2048]{1,0:T(8,128)(2,1)}, u32[]{:S(2)}) copy-start(bf16[256,2048]{1,0:T(8,128)(2,1)} %copy-done) | copy-start | bytes 3145732
Sparse Core Ops, SparseCore 0:
  10.2 26.8 all-gather.4
  39.2 22.9 all-gather.6
where the time goes:
time: 1130 us; the launch traced here: 1110 us
  waiting for transfers between devices  769 us (68%)
  local copies, waits for them, and re-layouts  137 us (12%)
  starting transfers between devices  94.2 us (8%)
  matrix products  49.4 us (4%)
  other arithmetic  48.9 us (4%)
  between operations  15.5 us (1%)
    all_to_all x1, waiting for transfers between devices, on_device(): lax.all_to_all(answers.reshape(n_experts, capacity, D), ('ctx', 'exp'), s...  383 us
    all_to_all x1, waiting for transfers between devices, on_device(): lax.all_to_all(outgoing.reshape(n_experts, capacity, D), ('ctx', 'exp'),...  357 us
    all_to_all x1, starting transfers between devices, on_device(): lax.all_to_all(answers.reshape(n_experts, capacity, D), ('ctx', 'exp'), s...  61 us
    gather x1, local copies, waits for them, and re-layouts, on_device(): packed = incoming[anchor]  39.3 us
    scatter x1, local copies, waits for them, and re-layouts, on_device(): jnp.zeros((n_experts * capacity, D), jnp.bfloat16).at[target]  33.4 us
    dot_general x3, matrix products, expert_rows(): lax.dot_general(hidden_rows, weights[2], (((1,), (1,)), ((), ())), prefer...  26.3 us
    all_to_all x1, starting transfers between devices, on_device(): lax.all_to_all(outgoing.reshape(n_experts, capacity, D), ('ctx', 'exp'),...  25.8 us
    all_gather x1, waiting for transfers between devices, on_device(): value_piece = lax.all_gather(values[0], 'ctx', axis=0, tiled=True)  25.1 us
  transfers between devices with their start and end apart: 5, of which 4 were waited for; matrix products, arithmetic and copies ran while one was open for 7% of the time, Pallas kernels for 0%

commit v1 on v0

v1 whole, which is shorter than its diff:
```python
import math

import jax
import jax.numpy as jnp
from jax import lax
from jax.experimental import pallas as pl
from jax.experimental.pallas import tpu as pltpu
from jax.sharding import PartitionSpec as P

D = 2048
HEADS = 16
KV_HEADS = 2
HEAD_DIM = 128
TOP = 8
GROUP = 512
ROUND_TOKENS = 8192


def attend(queries, keys, values):
    tok_rows = queries.shape[1]
    group_size = HEADS // KV_HEADS
    score_scale = 1.0 / math.sqrt(HEAD_DIM)
    query_heads = queries[0].reshape(tok_rows, KV_HEADS, group_size, HEAD_DIM)
    first_row = lax.axis_index("ctx") * tok_rows
    query_pos = first_row + jnp.arange(tok_rows, dtype=jnp.int32)
    last_row = first_row + tok_rows - 1
    running = (
        jnp.full((tok_rows, KV_HEADS, group_size), -1e30, jnp.float32),
        jnp.zeros((tok_rows, KV_HEADS, group_size), jnp.float32),
        jnp.zeros((tok_rows, KV_HEADS, group_size, HEAD_DIM), jnp.float32),
    )
    key_piece = lax.all_gather(keys[0], "ctx", axis=0, tiled=True)
    value_piece = lax.all_gather(values[0], "ctx", axis=0, tiled=True)
    piece_rows = key_piece.shape[0]
    absorb_block_rows = math.gcd(piece_rows, 512)

    def one_block(index, running):
        block_start = index * absorb_block_rows

        def compute(running):
            running_max, denom, accum = running
            key_rows = lax.dynamic_slice_in_dim(
                key_piece, block_start, absorb_block_rows, 0
            ).reshape(absorb_block_rows, KV_HEADS, HEAD_DIM)
            value_rows = lax.dynamic_slice_in_dim(
                value_piece, block_start, absorb_block_rows, 0
            ).reshape(absorb_block_rows, KV_HEADS, HEAD_DIM)
            scores = (
                jnp.einsum(
                    "tgjd,ngd->tgjn", query_heads, key_rows, preferred_element_type=jnp.float32
                )
                * score_scale
            )
            key_pos = block_start + jnp.arange(absorb_block_rows, dtype=jnp.int32)
            visible = (key_pos[None, :] <= query_pos[:, None])[:, None, None, :]
            scores = jnp.where(visible, scores, -1e30)
            new_max = jnp.maximum(running_max, scores.max(-1))
            exps = jnp.where(visible, jnp.exp(scores - new_max[..., None]), 0.0)
            rescale = jnp.exp(running_max - new_max)
            denom = denom * rescale + exps.sum(-1)
            added = jnp.einsum(
                "tgjn,ngd->tgjd",
                exps.astype(jnp.bfloat16),
                value_rows,
                preferred_element_type=jnp.float32,
            )
            accum = accum * rescale[..., None] + added
            return (new_max, denom, accum)

        return lax.cond(block_start <= last_row, compute, lambda state: state, running)

    running_max, denom, accum = lax.fori_loop(
        0, piece_rows // absorb_block_rows, one_block, running
    )
    return (accum / denom[..., None]).reshape(tok_rows, HEADS * HEAD_DIM).astype(jnp.bfloat16)


def expert_kernel(gate_ref, slot_ref, tok_ref, weight_ref, down_ref, out_ref):
    slots = slot_ref[0]
    rows = GROUP // 2
    chosen = slots == lax.broadcasted_iota(jnp.int32, (rows, GROUP), 0)
    row_gates = jnp.sum(jnp.where(chosen, gate_ref[0], 0.0), axis=1, keepdims=True)
    pick = chosen.astype(jnp.float32).astype(jnp.bfloat16)
    tokens = jnp.dot(pick, tok_ref[...], preferred_element_type=jnp.float32).astype(jnp.bfloat16)
    gate_part = jnp.dot(tokens, weight_ref[0, 0], preferred_element_type=jnp.float32)
    upper_part = jnp.dot(tokens, weight_ref[0, 1], preferred_element_type=jnp.float32)
    hidden = (gate_part / (1.0 + jnp.exp(-gate_part)) * upper_part).astype(jnp.bfloat16)
    result = jnp.dot(hidden, down_ref[...], preferred_element_type=jnp.float32)
    scaled = (result.astype(jnp.bfloat16).astype(jnp.float32) * row_gates).astype(jnp.bfloat16)
    out_ref[...] = lax.dot_general(
        pick, scaled, (((0,), (0,)), ((), ())), preferred_element_type=jnp.float32
    ).astype(jnp.bfloat16)


def expert_terms(tokens, gates, slots, weights, down):
    groups = tokens.shape[0] // GROUP
    ff = weights.shape[-1]
    return pl.pallas_call(
        expert_kernel,
        grid=(groups,),
        in_specs=[
            pl.BlockSpec((1, 1, GROUP), lambda i: (i, 0, 0)),
            pl.BlockSpec((1, 1, GROUP), lambda i: (i, 0, 0)),
            pl.BlockSpec((GROUP, D), lambda i: (i, 0)),
            pl.BlockSpec((1, 2, D, ff), lambda i: (0, 0, 0, 0)),
            pl.BlockSpec((ff, D), lambda i: (0, 0)),
        ],
        out_specs=pl.BlockSpec((GROUP, D), lambda i: (i, 0)),
        out_shape=jax.ShapeDtypeStruct(tokens.shape, jnp.bfloat16),
        compiler_params=pltpu.CompilerParams(vmem_limit_bytes=56 * 1024 * 1024),
        cost_estimate=pl.CostEstimate(
            flops=tokens.shape[0] * D * (3 * ff + 2 * GROUP),
            bytes_accessed=4 * tokens.size + 6 * D * ff,
            transcendentals=tokens.shape[0] * ff // 2,
        ),
    )(gates, slots, tokens, weights, down)


def on_device(
    queries, keys, values, hidden_in, out_proj, norm_gain, route_ids, route_scores, expert_weights
):
    tok_rows = queries.shape[1]
    both = ("ctx", "exp")
    n_dev = lax.axis_size("ctx") * lax.axis_size("exp")
    gates = jax.nn.softmax(route_scores[0], -1)
    named = route_ids[0][None, :, :] == jnp.arange(n_dev, dtype=jnp.int32)[:, None, None]
    by_expert = jnp.sum(jnp.where(named, gates[None], 0.0), -1)
    by_expert = jnp.where(jnp.any(named, -1), by_expert, -1.0)
    my_gates = lax.all_to_all(by_expert, both, split_axis=0, concat_axis=0, tiled=True)
    down = expert_weights[0, 2].T

    rounds = n_dev * tok_rows // ROUND_TOKENS
    part_rows = tok_rows // rounds
    groups = ROUND_TOKENS // GROUP
    round_gates = my_gates.reshape(n_dev, rounds, part_rows).transpose(1, 0, 2)
    round_gates = round_gates.reshape(rounds, groups, GROUP)
    mine = round_gates >= 0.0
    order = jnp.arange(GROUP)
    upto = (order[:, None] <= order[None, :]).astype(jnp.bfloat16)
    ranks = jnp.einsum(
        "rgt,tu->rgu", mine.astype(jnp.bfloat16), upto, preferred_element_type=jnp.float32
    )
    slots = jnp.where(mine, ranks.astype(jnp.int32) - 1, -1)[:, :, None, :]
    round_gates = round_gates[:, :, None, :]

    attended = attend(queries, keys, values)
    projected = jnp.dot(attended, out_proj, preferred_element_type=jnp.float32)
    residual = (hidden_in[0].astype(jnp.float32) + projected).astype(jnp.bfloat16)
    resid_f = residual.astype(jnp.float32)
    normed = (
        resid_f * lax.rsqrt(jnp.mean(resid_f * resid_f, -1, keepdims=True) + 1e-06) * norm_gain
    ).astype(jnp.bfloat16)

    def one_round(inputs):
        part, part_gates, part_slots = inputs
        tokens = lax.all_gather(part, both, axis=0, tiled=True)
        terms = expert_terms(tokens, part_gates, part_slots, expert_weights, down)
        return lax.psum_scatter(terms, both, scatter_dimension=0, tiled=True)

    parts = normed.reshape(rounds, part_rows, D)
    if rounds == 1:
        mixture = one_round((parts[0], round_gates[0], slots[0]))
    else:
        mixture = lax.map(one_round, (parts, round_gates, slots)).reshape(tok_rows, D)
    layer_out = (resid_f + mixture.astype(jnp.float32)).astype(jnp.bfloat16)
    return (residual[None], layer_out[None])


def solution(mesh):
    return jax.shard_map(
        on_device,
        mesh=mesh,
        in_specs=(
            P("exp", "ctx", None),
            P("exp", "ctx", None),
            P("exp", "ctx", None),
            P("exp", "ctx", None),
            P(),
            P(),
            P("exp", "ctx", None),
            P("exp", "ctx", None),
            P(("ctx", "exp"), None, None, None),
        ),
        out_specs=(P("exp", "ctx", None), P("exp", "ctx", None)),
        check_vma=False,
    )
```

time: 1130 us -> 1080 us (0.956); the launches traced: 1110 us -> 1080 us
  waiting for transfers between devices: 769 us -> 940 us
  local copies, waits for them, and re-layouts: 137 us -> 12 us
  starting transfers between devices: 94.2 us -> 25.9 us
  Pallas kernels: 0 us -> 65.9 us
  other arithmetic: 48.9 us -> 6.57 us
  matrix products: 49.4 us -> 10.4 us
    all_to_all x3 -> x1, waiting for transfers between devices: 739 us -> 4.13 us  [on_device(): lax.all_to_all(by_expert, both, split_axis=0, concat_axis=0, tiled=True)]
    reduce_scatter x0 -> x1, waiting for transfers between devices: none -> 706 us  [one_round(): return lax.psum_scatter(terms, both, scatter_dimension=0, tiled=True)]
    all_gather x2 -> x3, waiting for transfers between devices: 29.3 us -> 230 us  [the longest x1 181 us: one_round(): tokens = lax.all_gather(part, both, axis=0, tiled=True)]
    all_to_all x3 -> x1, starting transfers between devices: 94.1 us -> 25.5 us  [on_device(): lax.all_to_all(by_expert, both, split_axis=0, concat_axis=0, tiled=True)]
    pallas_call x0 -> x1, Pallas kernels: none -> 65.9 us  [expert_terms(): pl.pallas_call(expert_kernel, grid=(groups,), in_specs=[pl.BlockSpec((1,...]
    gather x4 -> x0, local copies, waits for them, and re-layouts: 64.9 us -> none  [the longest x1 39.3 us: on_device(): packed = incoming[anchor]]
    scatter x2 -> x0, local copies, waits for them, and re-layouts: 55.1 us -> none  [the longest x1 33.4 us: on_device(): jnp.zeros((n_experts * capacity, D), jnp.bfloat16).at[target]]
    dot_general x6 -> x1, matrix products: 39.2 us -> 0.18 us  [on_device(): jnp.einsum('rgt,tu->rgu', mine.astype(jnp.bfloat16), upto, preferred_elem...]
  transfers between devices with their start and end apart: 5 -> 5, of which waited for: 4 -> 5; matrix products, arithmetic and copies ran while one was open for 7% -> 1% of each run, Pallas kernels for 0% -> 0%
where the time goes in v1:
time: 1080 us
  waiting for transfers between devices  940 us (87%)
  Pallas kernels  65.9 us (6%)
  starting transfers between devices  25.9 us (2%)
  between operations  13.9 us (1%)
  local copies, waits for them, and re-layouts  12 us (1%)
    reduce_scatter x1, waiting for transfers between devices, one_round(): return lax.psum_scatter(terms, both, scatter_dimension=0, tiled=True)  706 us
    all_gather x1, waiting for transfers between devices, one_round(): tokens = lax.all_gather(part, both, axis=0, tiled=True)  181 us
    pallas_call x1, Pallas kernels, expert_terms(): pl.pallas_call(expert_kernel, grid=(groups,), in_specs=[pl.BlockSpec((1,...  65.9 us
    all_to_all x1, starting transfers between devices, on_device(): lax.all_to_all(by_expert, both, split_axis=0, concat_axis=0, tiled=True)  25.5 us
    all_gather x1, waiting for transfers between devices, attend(): value_piece = lax.all_gather(values[0], 'ctx', axis=0, tiled=True)  24.8 us
    all_gather x1, waiting for transfers between devices, attend(): key_piece = lax.all_gather(keys[0], 'ctx', axis=0, tiled=True)  24 us
  transfers between devices with their start and end apart: 5, of which 5 were waited for; matrix products, arithmetic and copies ran while one was open for 1% of the time, Pallas kernels for 0%

profile of v1, /device:TPU:0, one launch (start us, length us, event | category | flops | bytes accessed | tf_op | source)
XLA Modules:
  0.0 1075.1 jit_solution(694018111140157587)
XLA Ops:
  7.2 1.7 copy.45
  8.9 1.7 copy.47
  10.7 1.5 copy.46
  12.2 0.7 copy.48
  12.9 24.0 %all-gather.8.cloned.1.call-done = bf16[1,2048,256]{1,2,0:T(8,128)(2,1)} async-done(((bf16[1,256,256]{1,2,0:T(8,128)(2,1)}), bf16[1,2048,256]{1,2,0:T(8,128)(2,1)}) %all-gather.8.cloned.1.call-update) | async-done | bytes 1048592 | tf_op jit(solution)/shard_map/all_gather | solution.py:32
  36.9 24.8 %all-gather.10.cloned.1.call-done = bf16[1,2048,256]{1,2,0:T(8,128)(2,1)} async-done(((bf16[1,256,256]{1,2,0:T(8,128)(2,1)}), bf16[1,2048,256]{1,2,0:T(8,128)(2,1)}) %all-gather.10.cloned.1.call-update) | async-done | bytes 1048592 | tf_op jit(solution)/shard_map/all_gather | solution.py:33
  61.6 0.2 broadcast_in_dim.69
  61.9 7.7 while.18
  61.9 7.4 conditional.3
  61.9 0.1 broadcast_compare_fusion
  62.1 1.1 constant_dynamic-slice_fusion
  63.2 1.5 fusion.2
  64.7 2.0 fusion.4
  66.7 2.6 bitcast_add_fusion
  69.5 0.2 divide_convert_fusion
  69.8 6.1 fusion.14
  75.9 0.9 copy-done
  76.9 1.3 fusion.16
  78.2 0.1 fusion.21
  78.4 0.1 select_reduce_fusion
  78.5 0.6 copy.49
  79.1 25.5 %all-to-all-start = ((f32[32,1,256]{2,1,0:T(1,128)}), f32[32,1,256]{2,1,0:T(1,128)S(1)}, u32[]{:S(2)}, u32[]{:S(2)}) async-start(f32[32,1,256]{2,1,0:T(1,128)} %copy.49), calls=%async_computation | async-start | bytes 65536 | tf_op jit(solution)/shard_map/all_to_all | solution.py:129
  104.6 0.2 reduce-scatter.2.cloned.1.call-start
  104.9 3.0 copy.56
  107.8 4.1 all-to-all-done
  112.0 0.1 compare_reduce_fusion
  112.1 0.2 fusion.19
  112.3 0.6 squeeze_broadcast_in_dim.3.slot_ref
  112.9 181.2 %all-gather.6.cloned.1.call-done.tok_ref = bf16[8192,2048]{1,0:T(8,128)(2,1)} async-done(((bf16[256,2048]{1,0:T(8,128)(2,1)}), bf16[8192,2048]{1,0:T(8,128)(2,1)}) %all-gather.6.cloned.1.call-update) | async-done | bytes 33554448 | tf_op jit(solution)/shard_map/all_gather | solution.py:156
  294.1 65.9 %shard_map.104 = bf16[8192,2048]{1,0:T(8,128)(2,1)} custom-call(f32[16,1,512]{2,1,0:T(1,128)} %bitcast.64, s32[16,1,512]{2,1,0:T(1,128)} %squeeze_broadcast_in_dim.3.slot_ref, bf16[8192,2048]{1,0:T(8,128)(2,1)} %all-gather.6.cloned.1.call-done.tok_ref, bf16[1,3,2048,768]{3,2,1,0:T(8,128)(2,1)} %weight_ref.1, bf16[768,2048]{1,0:T(8,128)(2,1)} %bitcast.61), custom_call_target="tpu_custom_call" | custom-call | flops 55834574848 | bytes 76546048 | tf_op jit(solution)/shard_map/pallas_call | solution.py:98
  359.9 706.1 %reduce-scatter.2.cloned.1.call-done = bf16[256,2048]{1,0:T(8,128)(2,1)} async-done(((bf16[8192,2048]{1,0:T(8,128)(2,1)}), bf16[256,2048]{1,0:T(8,128)(2,1)}) %reduce-scatter.2.cloned.1.call-update) | async-done | bytes 1048592 | tf_op jit(solution)/shard_map/reduce_scatter | solution.py:158
  1066.0 2.6 fusion.20
  (40 shorter events, 0.4 us)
Async XLA Ops:
  7.2 29.7 %all-gather.8.cloned.1.call-start = ((), (), s32[]{:S(2)}) async-start(), calls=%async_computation.4 | async-start | bytes 1179648 | tf_op jit(solution)/shard_map/all_gather | solution.py:32
  8.9 52.7 %all-gather.10.cloned.1.call-start = ((), (), s32[]{:S(2)}) async-start(), calls=%async_computation.5 | async-start | bytes 1179648 | tf_op jit(solution)/shard_map/all_gather | solution.py:33
  10.6 283.4 %all-gather.6.cloned.1.call-start = ((), (), s32[]{:S(2)}) async-start(), calls=%async_computation.2 | async-start | bytes 34603008 | tf_op jit(solution)/shard_map/all_gather | solution.py:156
  69.7 7.1 copy-start.5
  69.7 8.4 copy-start.3
  69.8 8.5 copy-start.4
  75.9 1.0 copy-start
  75.9 28.9 %slice-start = ((bf16[1,3,2048,768]{3,2,1,0:T(8,128)(2,1)}), bf16[1,1,2048,768]{3,2,1,0:T(8,128)(2,1)S(1)}, s32[]{:S(2)}) async-start(bf16[1,3,2048,768]{3,2,1,0:T(8,128)(2,1)} %weight_ref.1), calls=%async_computation.6 | async-start | bytes 6291456 | tf_op jit(solution)/shard_map/slice | solution.py:130
  79.1 32.9 %all-to-all-start = ((f32[32,1,256]{2,1,0:T(1,128)}), f32[32,1,256]{2,1,0:T(1,128)S(1)}, u32[]{:S(2)}, u32[]{:S(2)}) async-start(f32[32,1,256]{2,1,0:T(1,128)} %copy.49), calls=%async_computation | async-start | bytes 65536 | tf_op jit(solution)/shard_map/all_to_all | solution.py:129
  104.6 961.4 %reduce-scatter.2.cloned.1.call-start = ((), (), s32[]{:S(2)}) async-start(), calls=%async_computation.3 | async-start | bytes 34603008 | tf_op jit(solution)/shard_map/reduce_scatter | solution.py:158
  111.9 182.1 %copy-start.2 = (f32[32,1,256]{2,1,0:T(1,128)}, f32[32,1,256]{2,1,0:T(1,128)S(1)}, u32[]{:S(2)}) copy-start(f32[32,1,256]{2,1,0:T(1,128)S(1)} %all-to-all-done) | copy-start | bytes 98308
  359.9 706.1 %copy-start.1 = (bf16[256,2048]{1,0:T(8,128)(2,1)S(1)}, bf16[256,2048]{1,0:T(8,128)(2,1)}, u32[]{:S(2)}) copy-start(bf16[256,2048]{1,0:T(8,128)(2,1)} %copy-done) | copy-start | bytes 3145732
Sparse Core Ops, SparseCore 0:
  10.2 26.6 all-gather.7
  39.0 22.5 all-gather.9
  78.3 215.7 all-gather.5
  360.1 705.9 reduce-scatter.1

commit v2 on v1

--- a/solution.py
+++ b/solution.py
@@ -116,6 +116,158 @@
     )(gates, slots, tokens, weights, down)
 
 
+def scatter_sum_kernel(term_ref, out_ref, held, own, first, second, from_z, load_sem, core_send,
+                       core_recv, first_send, first_recv, second_send, second_recv, z_send, z_recv):
+    ctx, exp = lax.axis_index("ctx"), lax.axis_index("exp")
+    z, core = ctx // 2, ctx % 2
+    y, x = exp // 2, exp % 2
+    beside_x, beside_y = y * 2 + (1 - x), (1 - y) * 2 + x
+    owners = (exp, beside_x, beside_y, (1 - y) * 2 + (1 - x))
+    sibling = (z * 2 + (1 - core), exp)
+    plane_peer = ((ctx, beside_x), (ctx, beside_y))
+    z_of = [(z + 1 + k) % 4 for k in range(4)]
+    z_peer = [(z_of[k] * 2 + core, exp) for k in range(3)]
+    rows, width = out_ref.shape
+    half = width // 2
+    columns = (pl.ds(0, half), pl.ds(half, half))
+    piece = min(rows, 32)
+
+    def remote(source, target, send, recv, device):
+        return pltpu.make_async_remote_copy(
+            src_ref=source, dst_ref=target, send_sem=send, recv_sem=recv,
+            device_id=device, device_id_type=pl.DeviceIdType.MESH,
+        )
+
+    def add_rows(target, one, other):
+        def some(i, carry):
+            part = pl.ds(pl.multiple_of(i * piece, piece), piece)
+            target[part, :] = one[part, :] + other[part, :]
+            return carry
+
+        lax.fori_loop(0, rows // piece, some, 0)
+
+    barrier = pltpu.get_barrier_semaphore()
+    partners = (sibling,) + plane_peer + tuple(z_peer)
+    for device in partners:
+        pl.semaphore_signal(barrier, inc=1, device_id=device, device_id_type=pl.DeviceIdType.MESH)
+    pl.semaphore_wait(barrier, len(partners))
+
+    loads, core_copies, first_copies, second_copies, z_copies = {}, {}, {}, {}, {}
+    for k in range(4):
+        for r in (3, 1, 2, 0):
+            slot = k * 4 + r
+            block = (z_of[k] * 2) * 4 + owners[r]
+            core_copies[slot] = remote(
+                term_ref.at[block + (1 - core) * 4], held.at[slot],
+                core_send.at[slot], core_recv.at[slot], sibling,
+            )
+            core_copies[slot].start()
+            loads[slot] = pltpu.make_async_copy(
+                term_ref.at[block + core * 4], own.at[slot], load_sem.at[slot]
+            )
+            loads[slot].start()
+
+    def send_first(k, h, j, r):
+        index = k * 4 + h * 2 + j
+        first_copies[index] = remote(
+            held.at[k * 4 + r, :, columns[h]], first.at[index],
+            first_send.at[index], first_recv.at[index], plane_peer[h],
+        )
+        first_copies[index].start()
+
+    def over_core(k):
+        for r in (3, 1, 2, 0):
+            slot = k * 4 + r
+            core_copies[slot].wait_recv()
+            loads[slot].wait()
+            add_rows(held.at[slot], held.at[slot], own.at[slot])
+            if r == 3:
+                send_first(k, 0, 1, 3)
+                send_first(k, 1, 1, 3)
+            elif r == 1:
+                send_first(k, 0, 0, 1)
+            elif r == 2:
+                send_first(k, 1, 0, 2)
+
+    def over_first(k):
+        for h in range(2):
+            index = k * 4 + h * 2 + 1
+            first_copies[index].wait_recv()
+            mine = held.at[k * 4 + 2 - h, :, columns[h]]
+            add_rows(first.at[index], first.at[index], mine)
+            place = k * 2 + h
+            second_copies[place] = remote(
+                first.at[index], second.at[place],
+                second_send.at[place], second_recv.at[place], plane_peer[1 - h],
+            )
+            second_copies[place].start()
+        for h in range(2):
+            index = k * 4 + h * 2
+            first_copies[index].wait_recv()
+            add_rows(first.at[index], first.at[index], held.at[k * 4, :, columns[h]])
+
+    def over_second(k):
+        for h in range(2):
+            second_copies[k * 2 + h].wait_recv()
+            total = own.at[k * 4, :, columns[h]]
+            add_rows(total, first.at[k * 4 + h * 2], second.at[k * 2 + h])
+        if k < 3:
+            z_copies[k] = remote(
+                own.at[k * 4], from_z.at[k], z_send.at[k], z_recv.at[k], z_peer[k]
+            )
+            z_copies[k].start()
+
+    for step in range(6):
+        if step < 4:
+            over_core(step)
+        if 1 <= step < 5:
+            over_first(step - 1)
+        if step >= 2:
+            over_second(step - 2)
+
+    for k in range(3):
+        z_copies[k].wait_recv()
+
+    def finish(i, carry):
+        part = pl.ds(pl.multiple_of(i * piece, piece), piece)
+        total = own[12, part, :].astype(jnp.float32)
+        for k in range(3):
+            total += from_z[k, part, :].astype(jnp.float32)
+        out_ref[part, :] = total.astype(jnp.bfloat16)
+        return carry
+
+    lax.fori_loop(0, rows // piece, finish, 0)
+    for copies in (core_copies, first_copies, second_copies, z_copies):
+        for copy in copies.values():
+            copy.wait_send()
+
+
+def scatter_sum(terms, n_ctx, n_exp):
+    if (n_ctx, n_exp) != (8, 4):
+        return lax.psum_scatter(terms, ("ctx", "exp"), scatter_dimension=0, tiled=True)
+    rows, width = terms.shape[0] // 32, terms.shape[1]
+    return pl.pallas_call(
+        scatter_sum_kernel,
+        out_shape=jax.ShapeDtypeStruct((rows, width), jnp.bfloat16),
+        in_specs=[pl.BlockSpec(memory_space=pl.ANY)],
+        out_specs=pl.BlockSpec(memory_space=pltpu.VMEM),
+        scratch_shapes=[
+            pltpu.VMEM((16, rows, width), jnp.bfloat16),
+            pltpu.VMEM((16, rows, width), jnp.bfloat16),
+            pltpu.VMEM((16, rows, width // 2), jnp.bfloat16),
+            pltpu.VMEM((8, rows, width // 2), jnp.bfloat16),
+            pltpu.VMEM((3, rows, width), jnp.bfloat16),
+        ]
+        + [pltpu.SemaphoreType.DMA((n,)) for n in (16, 16, 16, 16, 16, 8, 8, 3, 3)],
+        compiler_params=pltpu.CompilerParams(
+            collective_id=0, has_side_effects=True, vmem_limit_bytes=58 * 1024 * 1024
+        ),
+        cost_estimate=pl.CostEstimate(
+            flops=2 * terms.size, bytes_accessed=2 * terms.size, transcendentals=0
+        ),
+    )(terms.reshape(32, rows, width))
+
+
 def on_device(
     queries, keys, values, hidden_in, out_proj, norm_gain, route_ids, route_scores, expert_weights
 ):
@@ -155,7 +307,7 @@
         part, part_gates, part_slots = inputs
         tokens = lax.all_gather(part, both, axis=0, tiled=True)
         terms = expert_terms(tokens, part_gates, part_slots, expert_weights, down)
-        return lax.psum_scatter(terms, both, scatter_dimension=0, tiled=True)
+        return scatter_sum(terms, lax.axis_size("ctx"), lax.axis_size("exp"))
 
     parts = normed.reshape(rounds, part_rows, D)
     if rounds == 1:

time: 1080 us -> 538 us (0.50)
  waiting for transfers between devices: 940 us -> 234 us
  Pallas kernels: 65.9 us -> 235 us
    reduce_scatter x1 -> x0, waiting for transfers between devices: 706 us -> none  [one_round(): return lax.psum_scatter(terms, both, scatter_dimension=0, tiled=True)]
    pallas_call x0 -> x1, Pallas kernels: none -> 169 us  [scatter_sum(): pl.pallas_call(scatter_sum_kernel, out_shape=jax.ShapeDtypeStruct((rows,...]
  transfers between devices with their start and end apart: 5 -> 4, of which waited for: 5 -> 4; matrix products, arithmetic and copies ran while one was open for 1% -> 2% of each run, Pallas kernels for 0% -> 0%
where the time goes in v2:
time: 538 us
  Pallas kernels  235 us (44%)
  waiting for transfers between devices  234 us (43%)
  starting transfers between devices  25.8 us (5%)
  between operations  13.9 us (3%)
  local copies, waits for them, and re-layouts  12 us (2%)
  matrix products  10.4 us (2%)
  other arithmetic  6.57 us (1%)
    all_gather x1, waiting for transfers between devices, one_round(): tokens = lax.all_gather(part, both, axis=0, tiled=True)  181 us
    pallas_call x1, Pallas kernels, scatter_sum(): pl.pallas_call(scatter_sum_kernel, out_shape=jax.ShapeDtypeStruct((rows,...  169 us
    pallas_call x1, Pallas kernels, expert_terms(): pl.pallas_call(expert_kernel, grid=(groups,), in_specs=[pl.BlockSpec((1,...  65.9 us
    all_to_all x1, starting transfers between devices, on_device(): lax.all_to_all(by_expert, both, split_axis=0, concat_axis=0, tiled=True)  25.7 us
    all_gather x1, waiting for transfers between devices, attend(): value_piece = lax.all_gather(values[0], 'ctx', axis=0, tiled=True)  24.8 us
    all_gather x1, waiting for transfers between devices, attend(): key_piece = lax.all_gather(keys[0], 'ctx', axis=0, tiled=True)  24 us
  transfers between devices with their start and end apart: 4, of which 4 were waited for; matrix products, arithmetic and copies ran while one was open for 2% of the time, Pallas kernels for 0%

profile of v2, /device:TPU:0, one launch (start us, length us, event | category | flops | bytes accessed | tf_op | source)
XLA Modules:
  0.0 538.1 jit_solution(16239006121036316027)
XLA Ops:
  7.2 1.7 copy.45
  8.9 0.0 all-gather.10.cloned.1.call-start
  8.9 1.7 copy.47
  10.7 1.5 copy.46
  12.2 0.7 copy.48
  12.9 24.0 %all-gather.8.cloned.1.call-done = bf16[1,2048,256]{1,2,0:T(8,128)(2,1)} async-done(((bf16[1,256,256]{1,2,0:T(8,128)(2,1)}), bf16[1,2048,256]{1,2,0:T(8,128)(2,1)}) %all-gather.8.cloned.1.call-update) | async-done | bytes 1048592 | tf_op jit(solution)/shard_map/all_gather | solution.py:32
  36.9 24.8 %all-gather.10.cloned.1.call-done = bf16[1,2048,256]{1,2,0:T(8,128)(2,1)} async-done(((bf16[1,256,256]{1,2,0:T(8,128)(2,1)}), bf16[1,2048,256]{1,2,0:T(8,128)(2,1)}) %all-gather.10.cloned.1.call-update) | async-done | bytes 1048592 | tf_op jit(solution)/shard_map/all_gather | solution.py:33
  61.6 0.2 broadcast_in_dim.69
  61.9 7.7 %while.18 = (s32[]{:T(128)}, f32[256,2,8]{0,2,1:T(8,128)S(1)}, f32[256,2,8]{0,2,1:T(8,128)S(1)}, f32[256,2,8,128]{0,3,2,1:T(8,128)S(1)}, s32[]{:T(128)}, /*index...) while((s32[]{:T(128)}, f32[256,2,8]{0,2,1:T(8,128)S(1)}, ...), condition=%wide.region_5.6_spmd.clone, body=%wide.region_0.5_spmd.clone.sunk | while | flops 1102193408 | bytes 32776500 | solution.py:72
  61.9 7.4 %conditional.3 = ((f32[256,2,8]{0,2,1:T(8,128)S(1)}, f32[256,2,8]{0,2,1:T(8,128)S(1)}, f32[256,2,8,128]{0,3,2,1:T(8,128)S(1)})) conditional(s32[]{:T(128)} %convert_element_type.87, (f32[256,2,8]{0,2,1:T(8,128)S(1)}, f32[256,2,8]{0,2,1:T(8,128)S(1)}, f32[256,2,8,128]{0,3,2,1:T(8,128)S(1)}) %tuple.54, (s32[]{:T(128)}, s32[]{:T(128)}, ...), branch_computations={%region_1.1_spmd, %region_2.0_spmd} | conditional | flops 1102193408 | bytes 32775246 | solution.py:70
  61.9 0.1 broadcast_compare_fusion
  62.1 1.1 constant_dynamic-slice_fusion
  63.2 1.5 fusion.2
  64.7 2.0 fusion.4
  66.7 2.6 bitcast_add_fusion
  69.5 0.2 divide_convert_fusion
  69.8 6.1 %fusion.14 = (f32[256]{0:T(256)S(1)}, bf16[256,2048]{1,0:T(8,128)(2,1)S(1)}) fusion(bf16[256,2048]{0,1:T(8,128)(2,1)S(1)} %bitcast.60, bf16[2048,2048]{1,0:T(8,128)(2,1)} %param.17, bf16[1,256,2048]{2,1,0:T(8,128)(2,1)} %param.16), kind=kOutput, calls=%fused_computation.24 | convolution fusion | flops 2150629120 | bytes 11535360 | tf_op jit(solution)/shard_map/dot_general | solution.py:299
  75.9 0.9 copy-done
  76.9 1.3 fusion.16
  78.2 0.1 fusion.21
  78.4 0.1 select_reduce_fusion
  78.5 0.6 copy.49
  79.1 25.7 %all-to-all-start = ((f32[32,1,256]{2,1,0:T(1,128)}), f32[32,1,256]{2,1,0:T(1,128)S(1)}, u32[]{:S(2)}, u32[]{:S(2)}) async-start(f32[32,1,256]{2,1,0:T(1,128)} %copy.49), calls=%async_computation | async-start | bytes 65536 | tf_op jit(solution)/shard_map/all_to_all | solution.py:281
  104.8 3.0 copy.56
  107.8 4.2 all-to-all-done
  111.9 0.1 compare_reduce_fusion
  112.1 0.2 fusion.19
  112.3 0.6 squeeze_broadcast_in_dim.3.slot_ref
  112.9 181.2 %all-gather.6.cloned.1.call-done.tok_ref = bf16[8192,2048]{1,0:T(8,128)(2,1)} async-done(((bf16[256,2048]{1,0:T(8,128)(2,1)}), bf16[8192,2048]{1,0:T(8,128)(2,1)}) %all-gather.6.cloned.1.call-update) | async-done | bytes 33554448 | tf_op jit(solution)/shard_map/all_gather | solution.py:308
  294.1 65.9 %shard_map.104 = bf16[8192,2048]{1,0:T(8,128)(2,1)} custom-call(f32[16,1,512]{2,1,0:T(1,128)} %bitcast.66, s32[16,1,512]{2,1,0:T(1,128)} %squeeze_broadcast_in_dim.3.slot_ref, bf16[8192,2048]{1,0:T(8,128)(2,1)} %all-gather.6.cloned.1.call-done.tok_ref, bf16[1,3,2048,768]{3,2,1,0:T(8,128)(2,1)} %weight_ref.1, bf16[768,2048]{1,0:T(8,128)(2,1)} %bitcast.63), custom_call_target="tpu_custom_call" | custom-call | flops 55834574848 | bytes 76546048 | tf_op jit(solution)/shard_map/pallas_call | solution.py:98
  359.9 169.0 %shard_map.105 = bf16[256,2048]{1,0:T(8,128)(2,1)} custom-call(bf16[32,256,2048]{2,1,0:T(8,128)(2,1)} %bitcast.57), custom_call_target="tpu_custom_call" | custom-call | flops 33554432 | bytes 33554432 | tf_op jit(solution)/shard_map/pallas_call | solution.py:249
  528.9 2.6 fusion.20
  (38 shorter events, 0.3 us)
Async XLA Ops:
  7.2 29.7 %all-gather.8.cloned.1.call-start = ((), (), s32[]{:S(2)}) async-start(), calls=%async_computation.2 | async-start | bytes 1179648 | tf_op jit(solution)/shard_map/all_gather | solution.py:32
  8.9 52.7 %all-gather.10.cloned.1.call-start = ((), (), s32[]{:S(2)}) async-start(), calls=%async_computation.3 | async-start | bytes 1179648 | tf_op jit(solution)/shard_map/all_gather | solution.py:33
  10.6 283.4 %all-gather.6.cloned.1.call-start = ((), (), s32[]{:S(2)}) async-start(), calls=%async_computation.1 | async-start | bytes 34603008 | tf_op jit(solution)/shard_map/all_gather | solution.py:308
  69.7 7.1 %copy-start.5 = (f32[2048]{0:T(1024)S(1)}, f32[2048]{0:T(1024)}, u32[]{:S(2)}) copy-start(f32[2048]{0:T(1024)} %param.18) | copy-start | bytes 24580
  69.7 8.4 %copy-start.3 = (f32[1,256,8]{1,2,0:T(8,128)S(1)}, f32[1,256,8]{1,2,0:T(8,128)}, u32[]{:S(2)}) copy-start(f32[1,256,8]{1,2,0:T(8,128)} %param.20) | copy-start | bytes 24580
  69.8 8.5 %copy-start.4 = (s32[1,256,8]{1,2,0:T(8,128)S(1)}, s32[1,256,8]{1,2,0:T(8,128)}, u32[]{:S(2)}) copy-start(s32[1,256,8]{1,2,0:T(8,128)} %param.19) | copy-start | bytes 24580
  75.9 1.0 copy-start
  75.9 28.9 %slice-start = ((bf16[1,3,2048,768]{3,2,1,0:T(8,128)(2,1)}), bf16[1,1,2048,768]{3,2,1,0:T(8,128)(2,1)S(1)}, s32[]{:S(2)}) async-start(bf16[1,3,2048,768]{3,2,1,0:T(8,128)(2,1)} %weight_ref.1), calls=%async_computation.4 | async-start | bytes 6291456 | tf_op jit(solution)/shard_map/slice | solution.py:282
  79.1 32.9 %all-to-all-start = ((f32[32,1,256]{2,1,0:T(1,128)}), f32[32,1,256]{2,1,0:T(1,128)S(1)}, u32[]{:S(2)}, u32[]{:S(2)}) async-start(f32[32,1,256]{2,1,0:T(1,128)} %copy.49), calls=%async_computation | async-start | bytes 65536 | tf_op jit(solution)/shard_map/all_to_all | solution.py:281
  111.9 182.1 %copy-start.2 = (f32[32,1,256]{2,1,0:T(1,128)}, f32[32,1,256]{2,1,0:T(1,128)S(1)}, u32[]{:S(2)}) copy-start(f32[32,1,256]{2,1,0:T(1,128)S(1)} %all-to-all-done) | copy-start | bytes 98308
  359.9 169.0 %copy-start.1 = (bf16[256,2048]{1,0:T(8,128)(2,1)S(1)}, bf16[256,2048]{1,0:T(8,128)(2,1)}, u32[]{:S(2)}) copy-start(bf16[256,2048]{1,0:T(8,128)(2,1)} %copy-done) | copy-start | bytes 3145732
Sparse Core Ops, SparseCore 0:
  10.2 26.6 all-gather.7
  39.0 22.5 all-gather.9
  78.3 215.7 all-gather.5

commit v3 on v2

--- a/solution.py
+++ b/solution.py
@@ -29,8 +29,9 @@
         jnp.zeros((tok_rows, KV_HEADS, group_size), jnp.float32),
         jnp.zeros((tok_rows, KV_HEADS, group_size, HEAD_DIM), jnp.float32),
     )
-    key_piece = lax.all_gather(keys[0], "ctx", axis=0, tiled=True)
-    value_piece = lax.all_gather(values[0], "ctx", axis=0, tiled=True)
+    both_rows = jnp.concatenate([keys[0], values[0]], axis=1)
+    both_piece = lax.all_gather(both_rows, "ctx", axis=0, tiled=True)
+    key_piece, value_piece = jnp.split(both_piece, 2, axis=1)
     piece_rows = key_piece.shape[0]
     absorb_block_rows = math.gcd(piece_rows, 512)
 
@@ -242,10 +243,8 @@
             copy.wait_send()
 
 
-def scatter_sum(terms, n_ctx, n_exp):
-    if (n_ctx, n_exp) != (8, 4):
-        return lax.psum_scatter(terms, ("ctx", "exp"), scatter_dimension=0, tiled=True)
-    rows, width = terms.shape[0] // 32, terms.shape[1]
+def scatter_sum(terms):
+    rows, width = terms.shape[1:]
     return pl.pallas_call(
         scatter_sum_kernel,
         out_shape=jax.ShapeDtypeStruct((rows, width), jnp.bfloat16),
@@ -265,7 +264,203 @@
         cost_estimate=pl.CostEstimate(
             flops=2 * terms.size, bytes_accessed=2 * terms.size, transcendentals=0
         ),
-    )(terms.reshape(32, rows, width))
+    )(terms)
+
+
+def gather_expert_kernel(tok_ref, gate_ref, slot_ref, weight_ref, down_ref, term_ref,
+                         held, upper, down, picked, out, own_sem, weight_sem, out_sem,
+                         z_send, z_recv, side_send, side_recv, diag_send, diag_recv,
+                         core_send, core_recv):
+    ctx, exp = lax.axis_index("ctx"), lax.axis_index("exp")
+    z, core = ctx // 2, ctx % 2
+    y, x = exp // 2, exp % 2
+    beside_x, beside_y = y * 2 + (1 - x), (1 - y) * 2 + x
+    owners = (exp, beside_x, beside_y, (1 - y) * 2 + (1 - x))
+    sibling = (z * 2 + (1 - core), exp)
+    plane_peer = ((ctx, beside_x), (ctx, beside_y))
+    z_peer = [(((z + k) % 4) * 2 + core, exp) for k in (1, 2, 3)]
+    rows, width = tok_ref.shape
+    chunk = min(width, 512)
+    mine = pl.ds(pl.multiple_of(core * rows, rows), rows)
+    theirs = pl.ds(pl.multiple_of((1 - core) * rows, rows), rows)
+
+    def remote(source, target, send, recv, device):
+        return pltpu.make_async_remote_copy(
+            src_ref=source, dst_ref=target, send_sem=send, recv_sem=recv,
+            device_id=device, device_id_type=pl.DeviceIdType.MESH,
+        )
+
+    def z_copy(k):
+        return remote(tok_ref, held.at[k * 4, mine], z_send.at[k - 1], z_recv.at[k - 1],
+                      z_peer[k - 1])
+
+    def z_arrival(k):
+        return remote(tok_ref, held.at[k * 4, mine], z_send.at[k - 1], z_recv.at[k - 1],
+                      z_peer[0])
+
+    def side_copy(k, h):
+        return remote(held.at[k * 4, mine], held.at[k * 4 + 1 + h, mine],
+                      side_send.at[k * 2 + h], side_recv.at[k * 2 + h], plane_peer[h])
+
+    def diag_copy(k, h):
+        half = pl.ds(pl.multiple_of(core * rows + h * (rows // 2), rows // 2), rows // 2)
+        return remote(held.at[k * 4 + 2 - h, half], held.at[k * 4 + 3, half],
+                      diag_send.at[k * 2 + h], diag_recv.at[k * 2 + h], plane_peer[h])
+
+    def core_copy(k, r):
+        slot = k * 4 + r
+        return remote(held.at[slot, mine], held.at[slot, mine],
+                      core_send.at[slot], core_recv.at[slot], sibling)
+
+    def core_arrival(k, r):
+        slot = k * 4 + r
+        return remote(held.at[slot, theirs], held.at[slot, theirs],
+                      core_send.at[slot], core_recv.at[slot], sibling)
+
+    def out_copy(k, r, c):
+        block = (((z - k + 4) % 4) * 2 + c) * 4 + owners[r]
+        return pltpu.make_async_copy(
+            out.at[r % 2, pl.ds(c * rows, rows)], term_ref.at[block], out_sem.at[r % 2, c]
+        )
+
+    upper_load = pltpu.make_async_copy(weight_ref.at[0, pl.ds(0, 2)], upper, weight_sem.at[0])
+    down_load = pltpu.make_async_copy(down_ref, down, weight_sem.at[1])
+    own_load = pltpu.make_async_copy(tok_ref, held.at[0, mine], own_sem)
+    own_load.start()
+    upper_load.start()
+    down_load.start()
+
+    barrier = pltpu.get_barrier_semaphore()
+    partners = (sibling,) + plane_peer + tuple(z_peer)
+    for device in partners:
+        pl.semaphore_signal(barrier, inc=1, device_id=device, device_id_type=pl.DeviceIdType.MESH)
+    pl.semaphore_wait(barrier, len(partners))
+
+    def spread(k):
+        side_copy(k, 0).start()
+        side_copy(k, 1).start()
+        core_copy(k, 0).start()
+
+    own_load.wait()
+    spread(0)
+    for k in (1, 2, 3):
+        z_copy(k).start()
+    upper_load.wait()
+    down_load.wait()
+
+    def serve(k, r):
+        slot = k * 4 + r
+        core_arrival(k, r).wait_recv()
+        if r >= 2:
+            for c in range(2):
+                out_copy(k, r - 2, c).wait()
+        else:
+            @pl.when(k > 0)
+            def _():
+                for c in range(2):
+                    out_copy(k - 1, r + 2, c).wait()
+
+        group = ((z - k + 4) % 4) * 4 + owners[r]
+        chosen = slot_ref[group] == lax.broadcasted_iota(jnp.int32, (rows, 2 * rows), 0)
+        row_gates = jnp.sum(jnp.where(chosen, gate_ref[group], 0.0), axis=1, keepdims=True)
+        pick = chosen.astype(jnp.float32).astype(jnp.bfloat16)
+
+        def take(i, carry):
+            part = pl.ds(pl.multiple_of(i * chunk, chunk), chunk)
+            picked[:, part] = jnp.dot(
+                pick, held[slot, :, part], preferred_element_type=jnp.float32
+            ).astype(jnp.bfloat16)
+            return carry
+
+        lax.fori_loop(0, width // chunk, take, 0)
+        gate_part = jnp.dot(picked[...], upper[0], preferred_element_type=jnp.float32)
+        upper_part = jnp.dot(picked[...], upper[1], preferred_element_type=jnp.float32)
+        hidden = (gate_part / (1.0 + jnp.exp(-gate_part)) * upper_part).astype(jnp.bfloat16)
+
+        def give(i, carry):
+            part = pl.ds(pl.multiple_of(i * chunk, chunk), chunk)
+            result = jnp.dot(hidden, down[:, part], preferred_element_type=jnp.float32)
+            scaled = result.astype(jnp.bfloat16).astype(jnp.float32) * row_gates
+            out[r % 2, :, part] = lax.dot_general(
+                pick, scaled.astype(jnp.bfloat16), (((0,), (0,)), ((), ())),
+                preferred_element_type=jnp.float32,
+            ).astype(jnp.bfloat16)
+            return carry
+
+        lax.fori_loop(0, width // chunk, give, 0)
+        for c in range(2):
+            out_copy(k, r, c).start()
+
+    def step(k, carry):
+        serve(k, 0)
+        side_copy(k, 0).wait_recv()
+        diag_copy(k, 1).start()
+        core_copy(k, 1).start()
+        side_copy(k, 1).wait_recv()
+        diag_copy(k, 0).start()
+        core_copy(k, 2).start()
+        serve(k, 1)
+
+        @pl.when(k < 3)
+        def _():
+            z_arrival(k + 1).wait_recv()
+            spread(k + 1)
+
+        serve(k, 2)
+        diag_copy(k, 0).wait_recv()
+        diag_copy(k, 1).wait_recv()
+        core_copy(k, 3).start()
+        serve(k, 3)
+        return carry
+
+    lax.fori_loop(0, 4, step, 0)
+    for r in (2, 3):
+        for c in range(2):
+            out_copy(3, r, c).wait()
+    for k in (1, 2, 3):
+        z_copy(k).wait_send()
+
+    def drain(k, carry):
+        for h in range(2):
+            side_copy(k, h).wait_send()
+            diag_copy(k, h).wait_send()
+        for r in range(4):
+            core_copy(k, r).wait_send()
+        return carry
+
+    lax.fori_loop(0, 4, drain, 0)
+
+
+def gathered_terms(tokens, gates, slots, weights, down):
+    rows, width = tokens.shape
+    ff = weights.shape[-1]
+    vmem = pl.BlockSpec(memory_space=pltpu.VMEM)
+    hbm = pl.BlockSpec(memory_space=pl.ANY)
+    return pl.pallas_call(
+        gather_expert_kernel,
+        out_shape=jax.ShapeDtypeStruct((32, rows, width), jnp.bfloat16),
+        in_specs=[vmem, vmem, vmem, hbm, hbm],
+        out_specs=hbm,
+        scratch_shapes=[
+            pltpu.VMEM((16, 2 * rows, width), jnp.bfloat16),
+            pltpu.VMEM((2, width, ff), jnp.bfloat16),
+            pltpu.VMEM((ff, width), jnp.bfloat16),
+            pltpu.VMEM((rows, width), jnp.bfloat16),
+            pltpu.VMEM((2, 2 * rows, width), jnp.bfloat16),
+            pltpu.SemaphoreType.DMA,
+            pltpu.SemaphoreType.DMA((2,)),
+            pltpu.SemaphoreType.DMA((2, 2)),
+        ]
+        + [pltpu.SemaphoreType.DMA((n,)) for n in (3, 3, 8, 8, 8, 8, 16, 16)],
+        compiler_params=pltpu.CompilerParams(
+            collective_id=1, has_side_effects=True, vmem_limit_bytes=58 * 1024 * 1024
+        ),
+        cost_estimate=pl.CostEstimate(
+            flops=32 * rows * width * (3 * ff + 4 * rows),
+            bytes_accessed=64 * rows * width + 6 * width * ff,
+            transcendentals=16 * rows * ff,
+        ),
+    )(tokens, gates, slots, weights, down)
 
 
 def on_device(
@@ -281,10 +476,14 @@
     my_gates = lax.all_to_all(by_expert, both, split_axis=0, concat_axis=0, tiled=True)
     down = expert_weights[0, 2].T
 
+    kernel_mesh = (lax.axis_size("ctx"), lax.axis_size("exp")) == (8, 4)
     rounds = n_dev * tok_rows // ROUND_TOKENS
     part_rows = tok_rows // rounds
     groups = ROUND_TOKENS // GROUP
-    round_gates = my_gates.reshape(n_dev, rounds, part_rows).transpose(1, 0, 2)
+    if kernel_mesh:
+        round_gates = my_gates.reshape(4, 2, 4, tok_rows).transpose(0, 2, 1, 3)
+    else:
+        round_gates = my_gates.reshape(n_dev, rounds, part_rows).transpose(1, 0, 2)
     round_gates = round_gates.reshape(rounds, groups, GROUP)
     mine = round_gates >= 0.0
     order = jnp.arange(GROUP)
@@ -307,10 +506,13 @@
         part, part_gates, part_slots = inputs
         tokens = lax.all_gather(part, both, axis=0, tiled=True)
         terms = expert_terms(tokens, part_gates, part_slots, expert_weights, down)
-        return scatter_sum(terms, lax.axis_size("ctx"), lax.axis_size("exp"))
+        return lax.psum_scatter(terms, both, scatter_dimension=0, tiled=True)
 
     parts = normed.reshape(rounds, part_rows, D)
-    if rounds == 1:
+    if kernel_mesh:
+        terms = gathered_terms(normed, round_gates[0], slots[0], expert_weights, down)
+        mixture = scatter_sum(terms)
+    elif rounds == 1:
         mixture = one_round((parts[0], round_gates[0], slots[0]))
     else:
         mixture = lax.map(one_round, (parts, round_gates, slots)).reshape(tok_rows, D)

time: 538 us -> 440 us (0.82)
  waiting for transfers between devices: 234 us -> 10.3 us
  Pallas kernels: 235 us -> 367 us
  starting transfers between devices: 25.8 us -> 7.33 us
  local copies, waits for them, and re-layouts: 12 us -> 19.1 us
    all_gather x3 -> x1, waiting for transfers between devices: 230 us -> 10.3 us  [attend(): both_piece = lax.all_gather(both_rows, 'ctx', axis=0, tiled=True)]
    pallas_call x1, Pallas kernels: 65.9 us -> 180 us  [gathered_terms(): pl.pallas_call(gather_expert_kernel, out_shape=jax.ShapeDtypeStruct((32,...]
    all_to_all x1, starting transfers between devices: 25.7 us -> 7.3 us  [on_device(): lax.all_to_all(by_expert, both, split_axis=0, concat_axis=0, tiled=True)]
    pallas_call x1, Pallas kernels: 169 us -> 187 us  [scatter_sum(): pl.pallas_call(scatter_sum_kernel, out_shape=jax.ShapeDtypeStruct((rows,...]
  transfers between devices with their start and end apart: 4 -> 2, of which waited for: 4 -> 1; matrix products, arithmetic and copies ran while one was open for 2% -> 4% of each run, Pallas kernels for 0% -> 0%
where the time goes in v3:
time: 440 us; the launch traced here: 439 us
  Pallas kernels  367 us (83%)
  local copies, waits for them, and re-layouts  19.1 us (4%)
  between operations  14.2 us (3%)
  other arithmetic  10.8 us (2%)
  matrix products  10.4 us (2%)
  waiting for transfers between devices  10.3 us (2%)
  starting transfers between devices  7.33 us (2%)
    pallas_call x1, Pallas kernels, scatter_sum(): pl.pallas_call(scatter_sum_kernel, out_shape=jax.ShapeDtypeStruct((rows,...  187 us
    pallas_call x1, Pallas kernels, gathered_terms(): pl.pallas_call(gather_expert_kernel, out_shape=jax.ShapeDtypeStruct((32,...  180 us
    all_gather x1, waiting for transfers between devices, attend(): both_piece = lax.all_gather(both_rows, 'ctx', axis=0, tiled=True)  10.3 us
    unnamed x10, local copies, waits for them, and re-layouts  8.92 us
  transfers between devices with their start and end apart: 2, of which 1 were waited for; matrix products, arithmetic and copies ran while one was open for 4% of the time, Pallas kernels for 0%

profile of v3, /device:TPU:0, one launch (start us, length us, event | category | flops | bytes accessed | tf_op | source)
XLA Modules:
  0.0 439.0 jit_solution(5115419670596578985)
XLA Ops:
  7.2 1.0 copy.42
  8.2 1.0 copy.43
  9.2 0.7 pad_maximum_fusion
  10.0 0.7 reduce_max.18
  10.7 0.7 fusion.23
  11.4 0.8 fusion.21
  12.2 0.7 divide_bitcast_fusion
  12.9 0.8 select_reduce_fusion
  13.7 0.6 copy.46
  14.4 7.3 %all-to-all-start = ((f32[32,1,256]{2,1,0:T(1,128)}), f32[32,1,256]{2,1,0:T(1,128)S(1)}, u32[]{:S(2)}, u32[]{:S(2)}) async-start(f32[32,1,256]{2,1,0:T(1,128)} %copy.46), calls=%async_computation | async-start | bytes 65536 | tf_op jit(solution)/shard_map/all_to_all | solution.py:476
  21.7 1.5 copy.44
  23.2 0.7 copy.45
  23.8 3.8 slice.3
  27.6 4.7 %copy.56 = bf16[1,1,2048,768]{2,3,1,0:T(8,128)(2,1)} copy(bf16[1,1,2048,768]{3,2,1,0:T(8,128)(2,1)} %slice.3) | data formatting | bytes 6291456
  32.5 0.2 fusion.19
  32.7 0.6 squeeze_broadcast_in_dim.3.slot_ref
  33.3 0.6 squeeze_broadcast_in_dim_reshape.3.gate_ref
  34.0 10.3 %all-gather.2.cloned.1.call-done = bf16[2048,512]{0,1:T(8,128)(2,1)} async-done(((bf16[256,512]{0,1:T(8,128)(2,1)}), bf16[2048,512]{0,1:T(8,128)(2,1)}) %all-gather.2.cloned.1.call-update) | async-done | bytes 2097168 | tf_op jit(solution)/shard_map/all_gather | solution.py:33
  44.3 3.1 fusion.24
  47.4 0.2 broadcast_in_dim.69
  47.6 7.7 %while.18 = (s32[]{:T(128)}, f32[256,2,8]{0,2,1:T(8,128)S(1)}, f32[256,2,8]{0,2,1:T(8,128)S(1)}, f32[256,2,8,128]{0,3,2,1:T(8,128)S(1)}, s32[]{:T(128)}, /*index...) while((s32[]{:T(128)}, f32[256,2,8]{0,2,1:T(8,128)S(1)}, ...), condition=%wide.region_5.6_spmd.clone, body=%wide.region_0.5_spmd.clone.sunk | while | flops 1102193408 | bytes 32776500 | solution.py:73
  47.6 7.4 %conditional.3 = ((f32[256,2,8]{0,2,1:T(8,128)S(1)}, f32[256,2,8]{0,2,1:T(8,128)S(1)}, f32[256,2,8,128]{0,3,2,1:T(8,128)S(1)})) conditional(s32[]{:T(128)} %convert_element_type.87, (f32[256,2,8]{0,2,1:T(8,128)S(1)}, f32[256,2,8]{0,2,1:T(8,128)S(1)}, f32[256,2,8,128]{0,3,2,1:T(8,128)S(1)}) %tuple.55, (s32[]{:T(128)}, s32[]{:T(128)}, ...), branch_computations={%region_1.1_spmd, %region_2.0_spmd} | conditional | flops 1102193408 | bytes 32775246 | solution.py:71
  47.8 1.1 constant_dynamic-slice_fusion
  48.9 1.5 fusion.2
  50.4 2.0 fusion.4
  52.5 2.6 bitcast_add_fusion
  55.2 0.2 divide_convert_fusion
  55.5 6.1 %fusion.14 = (f32[256]{0:T(256)S(1)}, bf16[256,2048]{1,0:T(8,128)(2,1)S(1)}) fusion(bf16[256,2048]{0,1:T(8,128)(2,1)S(1)} %bitcast.62, bf16[2048,2048]{1,0:T(8,128)(2,1)} %param.17, bf16[1,256,2048]{2,1,0:T(8,128)(2,1)} %param.16), kind=kOutput, calls=%fused_computation.24 | convolution fusion | flops 2150629120 | bytes 11535360 | tf_op jit(solution)/shard_map/dot_general | solution.py:498
  61.6 1.3 fusion.16.tok_ref
  62.9 179.8 %shard_map.104.term_ref = bf16[32,256,2048]{2,1,0:T(8,128)(2,1)} custom-call(bf16[256,2048]{1,0:T(8,128)(2,1)} %fusion.16.tok_ref, f32[16,1,512]{2,1,0:T(1,128)} %squeeze_broadcast_in_dim_reshape.3.gate_ref, s32[16,1,512]{2,1,0:T(1,128)} %squeeze_broadcast_in_dim.3.slot_ref, bf16[1,3,2048,768]{3,2,1,0:T(8,128)(2,1)} %weight_ref.1, bf16[768,2048]{1,0:T(8,128)(2,1)} %bitcast.65), custom_call_target="tpu_custom_call" | custom-call | flops 55834574848 | bytes 42991616 | tf_op jit(solution)/shard_map/pallas_call | solution.py:439
  242.7 186.8 %shard_map.105 = bf16[256,2048]{1,0:T(8,128)(2,1)} custom-call(bf16[32,256,2048]{2,1,0:T(8,128)(2,1)} %shard_map.104.term_ref), custom_call_target="tpu_custom_call" | custom-call | flops 33554432 | bytes 33554432 | tf_op jit(solution)/shard_map/pallas_call | solution.py:248
  429.6 2.6 fusion.20
  (30 shorter events, 0.5 us)
Async XLA Ops:
  7.2 37.1 %all-gather.2.cloned.1.call-start = ((), (), s32[]{:S(2)}) async-start(), calls=%async_computation.1 | async-start | bytes 2359296 | tf_op jit(solution)/shard_map/all_gather | solution.py:33
  14.4 18.0 %all-to-all-start = ((f32[32,1,256]{2,1,0:T(1,128)}), f32[32,1,256]{2,1,0:T(1,128)S(1)}, u32[]{:S(2)}, u32[]{:S(2)}) async-start(f32[32,1,256]{2,1,0:T(1,128)} %copy.46), calls=%async_computation | async-start | bytes 65536 | tf_op jit(solution)/shard_map/all_to_all | solution.py:476
  55.5 6.1 %copy-start.1 = (f32[2048]{0:T(1024)S(1)}, f32[2048]{0:T(1024)}, u32[]{:S(2)}) copy-start(f32[2048]{0:T(1024)} %param.18) | copy-start | bytes 24580
  61.6 368.0 %copy-start = (bf16[256,2048]{1,0:T(8,128)(2,1)}, bf16[256,2048]{1,0:T(8,128)(2,1)S(1)}, u32[]{:S(2)}) copy-start(bf16[256,2048]{1,0:T(8,128)(2,1)S(1)} %get-tuple-element.288) | copy-start | bytes 3145732
Sparse Core Ops, SparseCore 0:
  10.2 34.0 all-gather.1

commit v4 on v3

--- a/solution.py
+++ b/solution.py
@@ -399,13 +399,13 @@
         side_copy(k, 1).wait_recv()
         diag_copy(k, 0).start()
         core_copy(k, 2).start()
-        serve(k, 1)
 
         @pl.when(k < 3)
         def _():
             z_arrival(k + 1).wait_recv()
             spread(k + 1)
 
+        serve(k, 1)
         serve(k, 2)
         diag_copy(k, 0).wait_recv()
         diag_copy(k, 1).wait_recv()

time: 440 us -> 444 us (level)
    pallas_call x1, Pallas kernels: 187 us -> 192 us  [scatter_sum(): pl.pallas_call(scatter_sum_kernel, out_shape=jax.ShapeDtypeStruct((rows,...]
where the time goes in v4:
time: 444 us
  Pallas kernels  371 us (84%)
  local copies, waits for them, and re-layouts  19.1 us (4%)
  between operations  14.2 us (3%)
  other arithmetic  10.8 us (2%)
  matrix products  10.4 us (2%)
  waiting for transfers between devices  10.3 us (2%)
  starting transfers between devices  7.33 us (2%)
    pallas_call x1, Pallas kernels, scatter_sum(): pl.pallas_call(scatter_sum_kernel, out_shape=jax.ShapeDtypeStruct((rows,...  192 us
    pallas_call x1, Pallas kernels, gathered_terms(): pl.pallas_call(gather_expert_kernel, out_shape=jax.ShapeDtypeStruct((32,...  179 us
    all_gather x1, waiting for transfers between devices, attend(): both_piece = lax.all_gather(both_rows, 'ctx', axis=0, tiled=True)  10.3 us
    unnamed x10, local copies, waits for them, and re-layouts  8.92 us
  transfers between devices with their start and end apart: 2, of which 1 were waited for; matrix products, arithmetic and copies ran while one was open for 4% of the time, Pallas kernels for 0%

profile of v4, /device:TPU:0, one launch (start us, length us, event | category | flops | bytes accessed | tf_op | source)
XLA Modules:
  0.0 443.6 jit_solution(7759662116807435155)
XLA Ops:
  7.2 1.0 copy.42
  8.2 1.0 copy.43
  9.2 0.7 pad_maximum_fusion
  10.0 0.7 reduce_max.18
  10.7 0.7 fusion.23
  11.4 0.8 fusion.21
  12.2 0.7 divide_bitcast_fusion
  12.9 0.8 select_reduce_fusion
  13.7 0.6 copy.46
  14.4 7.3 %all-to-all-start = ((f32[32,1,256]{2,1,0:T(1,128)}), f32[32,1,256]{2,1,0:T(1,128)S(1)}, u32[]{:S(2)}, u32[]{:S(2)}) async-start(f32[32,1,256]{2,1,0:T(1,128)} %copy.46), calls=%async_computation | async-start | bytes 65536 | tf_op jit(solution)/shard_map/all_to_all | solution.py:476
  21.7 1.5 copy.44
  23.2 0.7 copy.45
  23.8 3.8 slice.3
  27.6 4.7 %copy.56 = bf16[1,1,2048,768]{2,3,1,0:T(8,128)(2,1)} copy(bf16[1,1,2048,768]{3,2,1,0:T(8,128)(2,1)} %slice.3) | data formatting | bytes 6291456
  32.5 0.2 fusion.19
  32.7 0.6 squeeze_broadcast_in_dim.3.slot_ref
  33.3 0.6 squeeze_broadcast_in_dim_reshape.3.gate_ref
  34.0 10.3 %all-gather.2.cloned.1.call-done = bf16[2048,512]{0,1:T(8,128)(2,1)} async-done(((bf16[256,512]{0,1:T(8,128)(2,1)}), bf16[2048,512]{0,1:T(8,128)(2,1)}) %all-gather.2.cloned.1.call-update) | async-done | bytes 2097168 | tf_op jit(solution)/shard_map/all_gather | solution.py:33
  44.3 3.1 fusion.24
  47.4 0.2 broadcast_in_dim.69
  47.6 7.7 %while.18 = (s32[]{:T(128)}, f32[256,2,8]{0,2,1:T(8,128)S(1)}, f32[256,2,8]{0,2,1:T(8,128)S(1)}, f32[256,2,8,128]{0,3,2,1:T(8,128)S(1)}, s32[]{:T(128)}, /*index...) while((s32[]{:T(128)}, f32[256,2,8]{0,2,1:T(8,128)S(1)}, ...), condition=%wide.region_5.6_spmd.clone, body=%wide.region_0.5_spmd.clone.sunk | while | flops 1102193408 | bytes 32776500 | solution.py:73
  47.6 7.4 %conditional.3 = ((f32[256,2,8]{0,2,1:T(8,128)S(1)}, f32[256,2,8]{0,2,1:T(8,128)S(1)}, f32[256,2,8,128]{0,3,2,1:T(8,128)S(1)})) conditional(s32[]{:T(128)} %convert_element_type.87, (f32[256,2,8]{0,2,1:T(8,128)S(1)}, f32[256,2,8]{0,2,1:T(8,128)S(1)}, f32[256,2,8,128]{0,3,2,1:T(8,128)S(1)}) %tuple.55, (s32[]{:T(128)}, s32[]{:T(128)}, ...), branch_computations={%region_1.1_spmd, %region_2.0_spmd} | conditional | flops 1102193408 | bytes 32775246 | solution.py:71
  47.8 1.1 constant_dynamic-slice_fusion
  48.9 1.5 fusion.2
  50.4 2.0 fusion.4
  52.5 2.6 bitcast_add_fusion
  55.2 0.2 divide_convert_fusion
  55.5 6.1 %fusion.14 = (f32[256]{0:T(256)S(1)}, bf16[256,2048]{1,0:T(8,128)(2,1)S(1)}) fusion(bf16[256,2048]{0,1:T(8,128)(2,1)S(1)} %bitcast.62, bf16[2048,2048]{1,0:T(8,128)(2,1)} %param.17, bf16[1,256,2048]{2,1,0:T(8,128)(2,1)} %param.16), kind=kOutput, calls=%fused_computation.24 | convolution fusion | flops 2150629120 | bytes 11535360 | tf_op jit(solution)/shard_map/dot_general | solution.py:498
  61.6 1.3 fusion.16.tok_ref
  62.9 179.4 %shard_map.104.term_ref = bf16[32,256,2048]{2,1,0:T(8,128)(2,1)} custom-call(bf16[256,2048]{1,0:T(8,128)(2,1)} %fusion.16.tok_ref, f32[16,1,512]{2,1,0:T(1,128)} %squeeze_broadcast_in_dim_reshape.3.gate_ref, s32[16,1,512]{2,1,0:T(1,128)} %squeeze_broadcast_in_dim.3.slot_ref, bf16[1,3,2048,768]{3,2,1,0:T(8,128)(2,1)} %weight_ref.1, bf16[768,2048]{1,0:T(8,128)(2,1)} %bitcast.65), custom_call_target="tpu_custom_call" | custom-call | flops 55834574848 | bytes 42991616 | tf_op jit(solution)/shard_map/pallas_call | solution.py:439
  242.3 191.8 %shard_map.105 = bf16[256,2048]{1,0:T(8,128)(2,1)} custom-call(bf16[32,256,2048]{2,1,0:T(8,128)(2,1)} %shard_map.104.term_ref), custom_call_target="tpu_custom_call" | custom-call | flops 33554432 | bytes 33554432 | tf_op jit(solution)/shard_map/pallas_call | solution.py:248
  434.1 2.6 fusion.20
  (30 shorter events, 0.5 us)
Async XLA Ops:
  7.2 37.1 %all-gather.2.cloned.1.call-start = ((), (), s32[]{:S(2)}) async-start(), calls=%async_computation.1 | async-start | bytes 2359296 | tf_op jit(solution)/shard_map/all_gather | solution.py:33
  14.4 18.0 %all-to-all-start = ((f32[32,1,256]{2,1,0:T(1,128)}), f32[32,1,256]{2,1,0:T(1,128)S(1)}, u32[]{:S(2)}, u32[]{:S(2)}) async-start(f32[32,1,256]{2,1,0:T(1,128)} %copy.46), calls=%async_computation | async-start | bytes 65536 | tf_op jit(solution)/shard_map/all_to_all | solution.py:476
  55.5 6.1 %copy-start.1 = (f32[2048]{0:T(1024)S(1)}, f32[2048]{0:T(1024)}, u32[]{:S(2)}) copy-start(f32[2048]{0:T(1024)} %param.18) | copy-start | bytes 24580
  61.6 372.6 %copy-start = (bf16[256,2048]{1,0:T(8,128)(2,1)}, bf16[256,2048]{1,0:T(8,128)(2,1)S(1)}, u32[]{:S(2)}) copy-start(bf16[256,2048]{1,0:T(8,128)(2,1)S(1)} %get-tuple-element.288) | copy-start | bytes 3145732
Sparse Core Ops, SparseCore 0:
  10.2 34.0 all-gather.1
